TPU v7x, 256 devices: a whole 4x4x8 slice. The times are simulated.
256 devices in a mesh: row: 32 (over y, x, z_lo), col: 8 (over z_hi, core).
Axes of the slice: x: 4, y: 4, z: 8 (z_hi: 4, z_lo: 2; z = z_hi * 2 + z_lo), core: 2. Of those that a mesh axis runs over, the one named last changes fastest.
Arguments:
- matrix_tiles: float32 [32, 8, 32, 256, 256], P('row', 'col'), may hold values from -0.25 to 0.25
- tile_rows: int32 [32, 8, 32], P('row', 'col'), may hold values from 0 to 63, as said below
- tile_cols: int32 [32, 8, 32], P('row', 'col'), may hold values from 0 to 255, as said below
- tile_count: int32 [32, 8], P('row', 'col'), may hold values from 8 to 32, as said below
- link_tiles: float32 [32, 8, 8, 256, 256], P('row', 'col'), may hold values from -0.125 to 0.125
- link_rows: int32 [32, 8, 8], P('row', 'col'), may hold values from 0 to 63
- link_target: int32 [32, 8, 8], P('row', 'col'), may hold values from 0 to 7
- link_columns: int32 [8], replicated, may hold values from 0 to 2047, as said below
- objective: float32 [524288], P(('col', 'row')), may hold values from -16 to 16
- upper_bound: float32 [524288], P(('col', 'row')), may hold values from 0.25 to 4
- right_side: float32 [524288], P(('row', 'col')), may hold values from -16 to 16
- primal_start: float32 [524288], P(('col', 'row')), may hold values from 0 to 1
- dual_start: float32 [524288], P(('row', 'col')), may hold values from 0 to 1
- primal_weight: float32 [1], replicated, may hold values from 0.5 to 2
- step_start: float32 [1], replicated, may hold values from 2 to 4
Outputs:
- primal_out: float32 [524288], P(('col', 'row'))
- dual_out: float32 [524288], P(('row', 'col'))
- step_out: float32 [1], replicated
Inputs may be any that keep to these rules, and one draw needn't show every extreme that they name: Slots 0 to tile_count - 1 of a device are live and the others are to be ignored; at least one device has all 32 slots live. `tile_rows`: the live slots of one device name distinct tiles. `tile_cols`: the live slots of one device name distinct tiles. `link_columns`: distinct column tiles; the first and the last column tile are always among them.
All inputs are finite; a program needn't handle non-finite values.
Results may differ from a plain program's by a relative error of at most 0.0003.
Values sent between devices are 32-bit elements; how exact they have to be, the bound alone decides.
A program may use at most 64 MiB of HBM per device.

v0:
```python
import functools

import jax
import jax.numpy as jnp
from jax import lax
from jax.experimental import pallas as pl
from jax.experimental.pallas import tpu as pltpu
from jax.sharding import PartitionSpec as P

MESH = pl.DeviceIdType.MESH
F32 = jnp.float32
BF16 = jnp.bfloat16

NR = 32
NC = 8
T = 256
SLOTS = 32
LS = 8
GROUPS = 5
OWN = 16
XR = NR * OWN
YR = NC * OWN

PHASES = (
    [f"y{k}" for k in range(2)]
    + [f"x{k}" for k in range(3)]
    + [f"pull{k}" for k in range(2)]
    + [f"strip{k}" for k in range(2)]
    + [f"tab{k}" for k in range(3)]
    + [f"image{k}" for k in range(3)]
    + ["sum_col", "sum_z", "sum_yx", "last_z", "last_yx"]
)
PH = {name: i for i, name in enumerate(PHASES)}
CHUNK = 4 * T
CHUNKS = GROUPS * 8 * T // CHUNK
EARLY = 5


def dot(a, b):
    return lax.dot_general(a, b, (((1,), (0,)), ((), ())), preferred_element_type=F32)


def dot_t(a, b):
    return lax.dot_general(a, b, (((1,), (1,)), ((), ())), preferred_element_type=F32)


def two_parts(v):
    big = v.astype(BF16)
    return big, (v - big.astype(F32)).astype(BF16)


def side_by_side(v):
    big, small = two_parts(v)
    return jnp.concatenate([big, small], axis=1)


def placed(table, v):
    big, small = two_parts(v)
    rest = (v - big.astype(F32) - small.astype(F32)).astype(BF16)
    return dot(table, big) + dot(table, small) + dot(table, rest)


def stacked(p):
    big = p.astype(BF16).astype(F32)
    small = p - big
    return jnp.concatenate(
        [big[:, :128], big[:, 128:], small[:, :128], small[:, 128:]], axis=0
    ).astype(BF16)


def kernel(
    tiles,
    links,
    trow,
    tcol,
    cnt,
    lrow,
    ltgt,
    lcol,
    obj,
    ub,
    rhs,
    x0,
    y0,
    pw,
    st,
    x_out,
    y_out,
    s_out,
    landing,
    local,
    vectors,
    hi,
    lo,
    x0g,
    xg,
    yg,
    xpart,
    xsum,
    ypart,
    ysum,
    tab_s,
    tab_r,
    strip_s,
    strip_r,
    tot_s,
    tot_r,
    my_ref,
    mx_ref,
    gy_ref,
    gx_ref,
    gl_ref,
    ly_ref,
    lt_ref,
    lm_ref,
    picked,
    made,
    load_sem,
    small_sem,
    send_sem,
    recv_sem,
):
    r = lax.axis_index("row")
    c = lax.axis_index("col")
    ry, rx, rz = r // 8, (r // 2) % 4, r % 2
    ch, cc = c // 2, c % 2

    def row_peer(d):
        dy, dx, dz = d // 8, (d // 2) % 4, d % 2
        return (((ry + dy) % 4) * 4 + (rx + dx) % 4) * 2 + (rz + dz) % 2, c

    def row_back(d):
        dy, dx, dz = d // 8, (d // 2) % 4, d % 2
        return (((4 - dy) % 4) * 4 + (4 - dx) % 4) * 2 + dz

    def col_peer(d):
        return r, ((ch + d // 2) % 4) * 2 + (cc + d % 2) % 2

    def side_peer(d):
        dz, e = d // 8, d % 8
        return (ry * 4 + rx) * 2 + (rz + dz) % 2, col_peer(e)[1]

    def col_back(d):
        return ((4 - d // 2) % 4) * 2 + d % 2

    def send(name, peer, d, src, dst):
        k = PH[name]
        pltpu.make_async_remote_copy(
            src_ref=src,
            dst_ref=dst,
            send_sem=send_sem.at[k],
            recv_sem=recv_sem.at[k],
            device_id=peer(d),
            device_id_type=MESH,
        ).start()

    def send_all(name, peer, count, src_of, dst_of):
        def one(d, carry):
            send(name, peer, d, src_of(d), dst_of(d))
            return carry

        lax.fori_loop(1, count, one, 0)

    def slot(d, rows=OWN):
        return pl.ds(pl.multiple_of(d * rows, rows), rows)

    def total(name, ref):
        k = PH[name]
        return pltpu.make_async_remote_copy(
            src_ref=ref,
            dst_ref=ref,
            send_sem=send_sem.at[k],
            recv_sem=recv_sem.at[k],
            device_id=col_peer(1),
            device_id_type=MESH,
        )

    def arrived(name, ref):
        total(name, ref).wait_recv()

    pending = []

    barrier = pltpu.get_barrier_semaphore()
    def greet(peer):
        def one(d, carry):
            pl.semaphore_signal(barrier, inc=1, device_id=peer(d), device_id_type=MESH)
            return carry

        return one

    lax.fori_loop(1, 2 * NC, greet(side_peer), 0)
    lax.fori_loop(2, NR, greet(row_peer), 0)

    far = (y0, x0, ub, trow, tcol, cnt, lrow, ltgt, lcol, obj, rhs, pw, st)
    near = (
        yg.at[0, :OWN],
        x0g.at[0, :OWN],
        vectors.at[1],
        *local[:6],
        vectors.at[0],
        vectors.at[2],
        *local[6:],
    )
    small = [
        pltpu.make_async_copy(a, b, small_sem.at[i]) for i, (a, b) in enumerate(zip(far, near))
    ]
    for copy in small:
        copy.start()
    trow, tcol, cnt, lrow, ltgt, lcol, pw, st = local
    obj, ub, rhs = (vectors.at[i] for i in range(3))

    def load(i):
        rows = pl.ds(i * CHUNK, CHUNK)
        near_links = i * CHUNK - SLOTS * T
        src = tiles.at[rows] if near_links < 0 else links.at[pl.ds(near_links, CHUNK)]
        return pltpu.make_async_copy(src, landing.at[rows], load_sem.at[i])

    for i in range(EARLY):
        load(i).start()

    pl.semaphore_wait(barrier, 2 * NC + NR - 3)

    def gather_y(k, values=None):
        if values is not None:
            yg[k, :OWN] = values
        send_all(
            f"y{k}", col_peer, NC, lambda d: yg.at[k, :OWN], lambda d: yg.at[k, slot(col_back(d))]
        )
        pending.append((f"y{k}", yg.at[k, pl.ds(OWN, YR - OWN)]))

    def gather_x(k, values=None):
        if values is not None:
            xg[k, :OWN] = values
        send_all(
            f"x{k}", row_peer, NR, lambda d: xg.at[k, :OWN], lambda d: xg.at[k, slot(row_back(d))]
        )
        pending.append((f"x{k}", xg.at[k, pl.ds(OWN, XR - OWN)]))

    small[0].wait()
    gather_y(0)
    for i in range(EARLY, CHUNKS):
        load(i).start()

    def lanes(rows, count):
        shape = (rows, 4 * count)
        lane = lax.broadcasted_iota(jnp.int32, shape, 1)
        return lax.broadcasted_iota(jnp.int32, shape, 0), lane % count, (lane // count) % 2

    def four(v):
        return jnp.concatenate([v, v, v, v], axis=1)

    def dual_place(t):
        o = t >> 3
        rel = ((((o >> 1) - ch) & 3) << 1) | ((o - cc) & 1)
        return (rel << 3) | (t & 7)

    def primal_place(t):
        o = t >> 3
        rel = (
            ((((o >> 3) - ry) & 3) << 3) | ((((o >> 1) - rx) & 3) << 1) | ((o - rz) & 1)
        )
        return (rel << 3) | (t & 7)

    def one_hot(cond):
        return jnp.where(cond, 1.0, 0.0).astype(F32)

    for copy in small[1:]:
        copy.wait()
    row, s, h = lanes(XR, LS)
    spot = lcol[...] - c * (XR // 2)
    mine = (spot >= 0) & (spot < XR // 2)
    own = one_hot(row == 2 * four(jnp.where(mine, primal_place(spot), -8)) + h)
    own_here = jnp.transpose(own[:128])[: 2 * LS, :OWN].astype(BF16)
    x0g[0, OWN:] = placed(own_here, ub[...])
    send_all("x0", row_peer, NR, lambda d: x0g.at[0], lambda d: x0g.at[row_back(d)])
    pending.append(("x0", x0g.at[pl.ds(1, NR - 1)]))

    live = cnt[...]
    row, s, h = lanes(YR, SLOTS)
    my = one_hot((row == 2 * four(dual_place(trow[...])) + h) & (s < live))
    row, s, h = lanes(YR, LS)
    ly = one_hot(row == 2 * four(dual_place(lrow[...])) + h)
    row, s, h = lanes(XR, SLOTS)
    mx = one_hot((row == 2 * four(primal_place(tcol[...])) + h) & (s < live))
    own_pick = jnp.transpose(own)[: 2 * LS]
    own_pick_b = own_pick.astype(BF16)
    mx_b = mx.astype(BF16)
    both_here = dot(own_pick_b, mx_b)
    not_link = 1.0 - jnp.sum(own_pick, axis=0, keepdims=True)
    my_ref[...] = my.astype(BF16)
    mx_ref[...] = mx_b
    gy_ref[: 2 * SLOTS] = jnp.transpose(my)[: 2 * SLOTS].astype(BF16)
    gy_ref[2 * SLOTS :] = jnp.transpose(ly)[: 2 * LS].astype(BF16)
    gx_ref[: 2 * SLOTS] = (jnp.transpose(mx)[: 2 * SLOTS] * not_link).astype(BF16)
    gx_ref[2 * SLOTS :] = own_pick_b
    ly_ref[...] = ly.astype(BF16)
    row, s, h = lanes(2 * LS, LS)
    lt = one_hot(row == h * LS + four(ltgt[...]))
    gl_ref[: 2 * SLOTS] = jnp.transpose(both_here)[: 2 * SLOTS].astype(BF16)
    gl_ref[2 * SLOTS :] = jnp.transpose(lt)[: 2 * LS].astype(BF16)
    lt_ref[...] = lt.astype(BF16)
    lm_ref[...] = both_here.astype(BF16)
    here = own[:OWN, : 2 * LS].astype(BF16)
    link_row = jnp.sum(own[:OWN, : 2 * LS], axis=1, keepdims=True) > 0.0
    obj_link = placed(own_here, obj[...])

    for i in range(CHUNKS):
        load(i).wait()

        def split_tile(t, carry, i=i):
            rows = pl.ds(pl.multiple_of(i * CHUNK + t * T, T), T)
            big, small = two_parts(landing[rows])
            hi[rows] = big
            lo[rows] = small
            return carry

        lax.fori_loop(0, CHUNK // T, split_tile, 0)

    member = lax.broadcasted_iota(jnp.int32, (16, T), 0) % 8

    def halves(picks, count):
        left, right = picks[:count], picks[count:]
        big = jnp.concatenate([left[:, :128], right[:, :128]], axis=1)
        small = jnp.concatenate([left[:, 128:], right[:, 128:]], axis=1)
        return big, small

    def group(g, both, product):
        out = jnp.zeros((16, T), F32)
        for k in range(8):
            one = jnp.where(member == k, both, 0.0).astype(BF16)
            rows = pl.ds(pl.multiple_of((g * 8 + k) * T, T), T)
            out = out + product(one, hi[rows]) + product(one, lo[rows])
        return out[:8] + out[8:]

    def link_group(picks, product):
        return group(GROUPS - 1, jnp.concatenate(halves(picks, LS), axis=0), product)

    def main_groups(picks, product):
        big, small = halves(picks, SLOTS)
        for g in range(GROUPS - 1):
            picked[g, :8] = big[8 * g : 8 * g + 8]
            picked[g, 8:] = small[8 * g : 8 * g + 8]

        def one(g, carry):
            made[g] = group(g, picked[g], product)
            return carry

        lax.fori_loop(0, GROUPS - 1, one, 0)
        return made[...].reshape(SLOTS, T)

    def sum_slots(ref, k, first, slots):
        out = first
        for d in range(1, slots):
            out = out + ref[k, d * OWN : (d + 1) * OWN]
        return out

    def transpose_product(k, at_start=lambda: None, at_sent=lambda: None):
        arrived(f"y{k}", yg.at[k, pl.ds(OWN, YR - OWN)])
        at_start()
        picks = dot(gy_ref[...], side_by_side(yg[k]))
        main = stacked(main_groups(picks[: 2 * SLOTS], dot))
        xpart[k] = dot(mx_ref[...], main)
        send_all(
            f"pull{k}", row_peer, NR, lambda d: xpart.at[k, slot(d)], lambda d: xsum.at[k, slot(d)]
        )
        pending.append((f"pull{k}", xsum.at[k, pl.ds(OWN, XR - OWN)]))
        at_sent()
        link = stacked(link_group(picks[2 * SLOTS :], dot))
        strip_s[k] = dot(lt_ref[...], link) + dot(lm_ref[...], main) - obj_link
        send_all(
            f"strip{k}", row_peer, NR, lambda d: strip_s.at[k], lambda d: strip_r.at[k, slot(d)]
        )
        pending.append((f"strip{k}", strip_r.at[k, pl.ds(OWN, XR - OWN)]))

    def pull(k):
        arrived(f"pull{k}", xsum.at[k, pl.ds(OWN, XR - OWN)])
        return sum_slots(xsum, k, xpart[k, :OWN], NR)

    def share_table(k, table):
        tab_s[k][...] = table
        send_all(f"tab{k}", col_peer, NC, lambda d: tab_s[k], lambda d: tab_r[k].at[d])
        pending.append((f"tab{k}", tab_r[k].at[pl.ds(1, NC - 1)]))

    def shared_table(k):
        arrived(f"tab{k}", tab_r[k].at[pl.ds(1, NC - 1)])
        table = tab_s[k][...]
        for d in range(1, NC):
            table = table + tab_r[k][d]
        return table

    def share_links(k):
        arrived(f"strip{k}", strip_r.at[k, pl.ds(OWN, XR - OWN)])
        share_table(k + 1, sum_slots(strip_r, k, strip_s[k], NR))

    def link_pull(k):
        share_links(k)
        return shared_table(k + 1)

    def from_links(table):
        picks = dot(gl_ref[...], side_by_side(table))
        link = link_group(picks[2 * SLOTS :], dot_t)
        return picks[: 2 * SLOTS], dot(ly_ref[...], stacked(link))

    def forward_product(k, vector, picks, strips):
        picks = picks + dot(gx_ref[: 2 * SLOTS], side_by_side(vector))
        main = dot(my_ref[...], stacked(main_groups(picks, dot_t)))
        ypart[k] = main + strips
        send_all(
            f"image{k}", col_peer, NC, lambda d: ypart.at[k, slot(d)], lambda d: ysum.at[k, slot(d)]
        )
        pending.append((f"image{k}", ysum.at[k, pl.ds(OWN, YR - OWN)]))

    def gathered_x(k):
        arrived(f"x{k}", xg.at[k, pl.ds(OWN, XR - OWN)])
        return xg[k]

    def image(k):
        arrived(f"image{k}", ysum.at[k, pl.ds(OWN, YR - OWN)])
        return sum_slots(ysum, k, ypart[k, :OWN], NC)

    weight = pw[...]
    step = st[...]

    def next_primal(now, step, pulled):
        return jnp.clip(now - (step / weight) * (obj[...] - pulled), 0.0, ub[...])

    def next_dual(now, step, old, new):
        return jnp.maximum(now + (step * weight) * (rhs[...] - 2.0 * new + old), 0.0)

    def sums(dx, dy, di):
        rows = [jnp.sum(v, axis=0, keepdims=True) for v in (dx * dx, dy * dy, dy * di)]
        return jnp.concatenate(rows + [jnp.zeros((5, 128), F32)], axis=0)

    def spread(name, first, value, peers, src):
        peer, count = peers
        tot_s[src] = value
        send_all(
            name, peer, count, lambda d: tot_s.at[src], lambda d: tot_r.at[slot(first + d - 1, 8)]
        )
        pending.append((name, tot_r.at[pl.ds(first * 8, (count - 1) * 8)]))

    def collect(name, first, value, count):
        arrived(name, tot_r.at[pl.ds(first * 8, count * 8)])
        for i in range(count):
            value = value + tot_r[(first + i) * 8 : (first + i + 1) * 8]
        return value

    col_peers = (col_peer, NC)
    z_peers = (row_peer, 2)
    yx_peers = (lambda d: row_peer(2 * d), NR // 2)
    side_peers = (side_peer, 2 * NC)

    def next_step(step, totals, iteration):
        lanes_summed = jnp.sum(totals, axis=1, keepdims=True)
        primal, dual, cross = lanes_summed[0:1], lanes_summed[1:2], lanes_summed[2:3]
        weighted = weight * primal + dual / weight + 1e-6
        shrink = 1.0 - (iteration + 2.0) ** (-0.3)
        growth = 1.0 + (iteration + 2.0) ** (-0.6)
        return (
            shrink
            * weighted
            / jnp.maximum(2.0 * jnp.abs(cross), shrink * weighted / (growth * step))
        )

    transpose_product(0)
    arrived("x0", x0g.at[pl.ds(1, NR - 1)])
    start = x0g[...]
    vector = start[:, :OWN].reshape(XR, 128)
    table = dot(own_pick_b, side_by_side(vector))
    share_table(
        0,
        jnp.concatenate([table[:, :128] + table[:, 128:], jnp.sum(start[:, OWN:], axis=0)], 0),
    )

    def next_links(now, step, pulled):
        return jnp.clip(now + (step / weight) * pulled, 0.0, ub_link)

    def patched(x, links):
        return jnp.where(link_row, placed(here, links), x)

    x_now = x0g[0, :OWN]
    y_now = yg[0, :OWN]
    x_next = next_primal(x_now, step, pull(0))
    gather_x(1, x_next)
    table = shared_table(0)
    x_link, ub_link = table[:OWN], table[OWN:]
    share_links(0)
    forward_product(0, vector, *from_links(x_link))
    x_link = next_links(x_link, step, shared_table(1))
    beside = from_links(x_link)
    x_next = patched(x_next, x_link)
    forward_product(1, gathered_x(1), *beside)
    image_old = image(0)
    image_new = image(1)
    y_next = next_dual(y_now, step, image_old, image_new)
    gather_y(1, y_next)
    value = sums(x_next - x_now, y_next - y_now, image_new - image_old)
    spread("sum_col", 0, value, col_peers, 0)
    x_now, y_now, image_old = x_next, y_next, image_new

    def at_start():
        spread("sum_z", 7, collect("sum_col", 0, value, 7), z_peers, 1)

    def at_sent():
        spread("sum_yx", 8, collect("sum_z", 7, tot_s[1], 1), yx_peers, 2)

    transpose_product(1, at_start, at_sent)
    step = next_step(step, collect("sum_yx", 8, tot_s[2], 15), 0)
    x_next = next_primal(x_now, step, pull(1))
    gather_x(2, x_next)
    x_link = next_links(x_link, step, link_pull(1))
    beside = from_links(x_link)
    x_next = patched(x_next, x_link)
    x_out[...] = x_next
    forward_product(2, gathered_x(2), *beside)
    image_new = image(2)
    y_next = next_dual(y_now, step, image_old, image_new)
    y_out[...] = y_next
    value = sums(x_next - x_now, y_next - y_now, image_new - image_old)
    spread("last_z", 23, value, side_peers, 3)
    value = collect("last_z", 23, value, 15)
    spread("last_yx", 38, value, yx_peers, 4)
    value = collect("last_yx", 38, value, 15)
    s_out[...] = next_step(step, value, 1)

    for name, ref in pending:
        total(name, ref).wait_send()


def on_device(
    matrix_tiles,
    tile_rows,
    tile_cols,
    tile_count,
    link_tiles,
    link_rows,
    link_target,
    link_columns,
    objective,
    upper_bound,
    right_side,
    primal_start,
    dual_start,
    primal_weight,
    step_start,
):
    flat = lambda v: v.reshape(OWN, 128)
    vmem = pl.BlockSpec(memory_space=pltpu.VMEM)
    hbm = pl.BlockSpec(memory_space=pltpu.HBM)
    n = len(PHASES)
    x, y, s = pl.pallas_call(
        kernel,
        out_shape=(
            jax.ShapeDtypeStruct((OWN, 128), F32),
            jax.ShapeDtypeStruct((OWN, 128), F32),
            jax.ShapeDtypeStruct((1, 1), F32),
        ),
        in_specs=[hbm] * 15,
        out_specs=(vmem, vmem, vmem),
        scratch_shapes=[
            pltpu.VMEM((GROUPS * 8 * T, T), F32),
            [pltpu.VMEM((1, m), jnp.int32) for m in (SLOTS, SLOTS, 1, LS, LS, LS)]
            + [pltpu.VMEM((1, 1), F32)] * 2,
            pltpu.VMEM((3, OWN, 128), F32),
            pltpu.VMEM((GROUPS * 8 * T, T), BF16),
            pltpu.VMEM((GROUPS * 8 * T, T), BF16),
            pltpu.VMEM((NR, 2 * OWN, 128), F32),
            pltpu.VMEM((3, XR, 128), F32),
            pltpu.VMEM((2, YR, 128), F32),
            pltpu.VMEM((2, XR, 128), F32),
            pltpu.VMEM((2, XR, 128), F32),
            pltpu.VMEM((3, YR, 128), F32),
            pltpu.VMEM((3, YR, 128), F32),
            [pltpu.VMEM((m * OWN, 128), F32) for m in (2, 1, 1)],
            [pltpu.VMEM((NC, m * OWN, 128), F32) for m in (2, 1, 1)],
            pltpu.VMEM((2, OWN, 128), F32),
            pltpu.VMEM((2, XR, 128), F32),
            pltpu.VMEM((5, 8, 128), F32),
            pltpu.VMEM((53 * 8, 128), F32),
            pltpu.VMEM((YR, 128), BF16),
            pltpu.VMEM((XR, 128), BF16),
            pltpu.VMEM((80, YR), BF16),
            pltpu.VMEM((80, XR), BF16),
            pltpu.VMEM((80, 16), BF16),
            pltpu.VMEM((YR, 32), BF16),
            pltpu.VMEM((16, 32), BF16),
            pltpu.VMEM((16, 128), BF16),
            pltpu.VMEM((GROUPS - 1, 16, T), F32),
            pltpu.VMEM((GROUPS - 1, 8, T), F32),
            pltpu.SemaphoreType.DMA((CHUNKS,)),
            pltpu.SemaphoreType.DMA((13,)),
            pltpu.SemaphoreType.DMA((n,)),
            pltpu.SemaphoreType.DMA((n,)),
        ],
        compiler_params=pltpu.CompilerParams(
            collective_id=0, has_side_effects=True, vmem_limit_bytes=63 * 1024 * 1024
        ),
        name="pdhg",
    )(
        matrix_tiles.reshape(SLOTS * T, T),
        link_tiles.reshape(LS * T, T),
        tile_rows.reshape(1, SLOTS),
        tile_cols.reshape(1, SLOTS),
        tile_count.reshape(1, 1),
        link_rows.reshape(1, LS),
        link_target.reshape(1, LS),
        link_columns.reshape(1, LS),
        flat(objective),
        flat(upper_bound),
        flat(right_side),
        flat(primal_start),
        flat(dual_start),
        primal_weight.reshape(1, 1),
        step_start.reshape(1, 1),
    )
    return x.reshape(-1), y.reshape(-1), s.reshape(1)


def solution(mesh):
    tile = P("row", "col", None, None, None)
    index = P("row", "col", None)
    primal = P(("col", "row"))
    dual = P(("row", "col"))
    return jax.shard_map(
        on_device,
        mesh=mesh,
        in_specs=(
            tile,
            index,
            index,
            P("row", "col"),
            tile,
            index,
            index,
            P(),
            primal,
            primal,
            dual,
            primal,
            dual,
            P(),
            P(),
        ),
        out_specs=(primal, dual, P()),
        check_vma=False,
    )
```

profile of v0, /device:TPU:1, one launch (start us, length us, event | category | flops | bytes accessed | tf_op | source)
XLA Modules:
  0.0 94.6 jit_solution(381280028931083523)
XLA Ops:
  2.6 87.6 %pdhg.1 = (f32[16,128]{1,0:T(8,128)}, f32[16,128]{1,0:T(8,128)}, f32[1,1]{1,0:T(1,128)}) custom-call(f32[8192,256]{1,0:T(8,128)} %bitcast.19, f32[2048,256]{1,0:T(8,128)} %bitcast.20, s32[1,32]{1,0:T(1,128)} %bitcast.28, s32[1,32]{1,0:T(1,128)} %bitcast.29, s32[1,1]{1,0:T(1,128)S(6)} %copy.21.cnt, s32[1,8]{1,0:T(1,128)} %bitcast.30, s32[1,8]{1,0:T(1,128)} %bitcast.31, ...), custom_call_target="tpu_custom_call" | custom-call | tf_op jit(solution)/shard_map/pdhg/pallas_call | solution.py:551
  90.2 1.3 %copy.24 = f32[2048]{0:T(1024)} copy(f32[2048]{0:T(1024)} %bitcast.22) | data formatting | bytes 16384
  91.5 1.3 %copy.25 = f32[2048]{0:T(1024)} copy(f32[2048]{0:T(1024)} %bitcast.21) | data formatting | bytes 16384
where the time goes:
time: 94.8 us; the launch traced here: 94.6 us
  Pallas kernels  87.6 us (92%)
  between operations  4.34 us (5%)
  local copies, waits for them, and re-layouts  2.59 us (3%)
    pallas_call x1, Pallas kernels, on_device(): pl.pallas_call(kernel, out_shape=(jax.ShapeDtypeStruct((OWN, 128), F32),...  87.6 us
    unnamed x2, local copies, waits for them, and re-layouts  2.59 us

commit v1 on v0

--- a/solution.py
+++ b/solution.py
@@ -28,7 +28,7 @@
     + [f"strip{k}" for k in range(2)]
     + [f"tab{k}" for k in range(3)]
     + [f"image{k}" for k in range(3)]
-    + ["sum_col", "sum_z", "sum_yx", "last_z", "last_yx"]
+    + ["sum_col", "sum_row", "last_z", "last_yx"]
 )
 PH = {name: i for i, name in enumerate(PHASES)}
 CHUNK = 4 * T
@@ -38,10 +38,6 @@
 
 def dot(a, b):
     return lax.dot_general(a, b, (((1,), (0,)), ((), ())), preferred_element_type=F32)
-
-
-def dot_t(a, b):
-    return lax.dot_general(a, b, (((1,), (1,)), ((), ())), preferred_element_type=F32)
 
 
 def two_parts(v):
@@ -92,6 +88,8 @@
     vectors,
     hi,
     lo,
+    hi_t,
+    lo_t,
     x0g,
     xg,
     yg,
@@ -115,6 +113,7 @@
     lm_ref,
     picked,
     made,
+    results,
     load_sem,
     small_sem,
     send_sem,
@@ -324,25 +323,25 @@
         small = jnp.concatenate([left[:, 128:], right[:, 128:]], axis=1)
         return big, small
 
-    def group(g, both, product):
+    def group(g, both, parts):
         out = jnp.zeros((16, T), F32)
         for k in range(8):
             one = jnp.where(member == k, both, 0.0).astype(BF16)
             rows = pl.ds(pl.multiple_of((g * 8 + k) * T, T), T)
-            out = out + product(one, hi[rows]) + product(one, lo[rows])
+            out = out + dot(one, parts[0][rows]) + dot(one, parts[1][rows])
         return out[:8] + out[8:]
 
-    def link_group(picks, product):
-        return group(GROUPS - 1, jnp.concatenate(halves(picks, LS), axis=0), product)
-
-    def main_groups(picks, product):
+    def link_group(picks, parts):
+        return group(GROUPS - 1, jnp.concatenate(halves(picks, LS), axis=0), parts)
+
+    def main_groups(picks, parts):
         big, small = halves(picks, SLOTS)
         for g in range(GROUPS - 1):
             picked[g, :8] = big[8 * g : 8 * g + 8]
             picked[g, 8:] = small[8 * g : 8 * g + 8]
 
         def one(g, carry):
-            made[g] = group(g, picked[g], product)
+            made[g] = group(g, picked[g], parts)
             return carry
 
         lax.fori_loop(0, GROUPS - 1, one, 0)
@@ -354,18 +353,17 @@
             out = out + ref[k, d * OWN : (d + 1) * OWN]
         return out
 
-    def transpose_product(k, at_start=lambda: None, at_sent=lambda: None):
+    def transpose_product(k, at_start=lambda: None):
         arrived(f"y{k}", yg.at[k, pl.ds(OWN, YR - OWN)])
         at_start()
         picks = dot(gy_ref[...], side_by_side(yg[k]))
-        main = stacked(main_groups(picks[: 2 * SLOTS], dot))
+        main = stacked(main_groups(picks[: 2 * SLOTS], (hi, lo)))
         xpart[k] = dot(mx_ref[...], main)
         send_all(
             f"pull{k}", row_peer, NR, lambda d: xpart.at[k, slot(d)], lambda d: xsum.at[k, slot(d)]
         )
         pending.append((f"pull{k}", xsum.at[k, pl.ds(OWN, XR - OWN)]))
-        at_sent()
-        link = stacked(link_group(picks[2 * SLOTS :], dot))
+        link = stacked(link_group(picks[2 * SLOTS :], (hi, lo)))
         strip_s[k] = dot(lt_ref[...], link) + dot(lm_ref[...], main) - obj_link
         send_all(
             f"strip{k}", row_peer, NR, lambda d: strip_s.at[k], lambda d: strip_r.at[k, slot(d)]
@@ -398,12 +396,12 @@
 
     def from_links(table):
         picks = dot(gl_ref[...], side_by_side(table))
-        link = link_group(picks[2 * SLOTS :], dot_t)
+        link = link_group(picks[2 * SLOTS :], (hi_t, lo_t))
         return picks[: 2 * SLOTS], dot(ly_ref[...], stacked(link))
 
     def forward_product(k, vector, picks, strips):
         picks = picks + dot(gx_ref[: 2 * SLOTS], side_by_side(vector))
-        main = dot(my_ref[...], stacked(main_groups(picks, dot_t)))
+        main = dot(my_ref[...], stacked(main_groups(picks, (hi_t, lo_t))))
         ypart[k] = main + strips
         send_all(
             f"image{k}", col_peer, NC, lambda d: ypart.at[k, slot(d)], lambda d: ysum.at[k, slot(d)]
@@ -446,7 +444,6 @@
         return value
 
     col_peers = (col_peer, NC)
-    z_peers = (row_peer, 2)
     yx_peers = (lambda d: row_peer(2 * d), NR // 2)
     side_peers = (side_peer, 2 * NC)
 
@@ -471,6 +468,13 @@
         0,
         jnp.concatenate([table[:, :128] + table[:, 128:], jnp.sum(start[:, OWN:], axis=0)], 0),
     )
+    def turn_tile(t, carry):
+        rows = pl.ds(pl.multiple_of(t * T, T), T)
+        hi_t[rows] = jnp.transpose(hi[rows])
+        lo_t[rows] = jnp.transpose(lo[rows])
+        return carry
+
+    lax.fori_loop(0, GROUPS * 8, turn_tile, 0)
 
     def next_links(now, step, pulled):
         return jnp.clip(now + (step / weight) * pulled, 0.0, ub_link)
@@ -499,30 +503,33 @@
     x_now, y_now, image_old = x_next, y_next, image_new
 
     def at_start():
-        spread("sum_z", 7, collect("sum_col", 0, value, 7), z_peers, 1)
-
-    def at_sent():
-        spread("sum_yx", 8, collect("sum_z", 7, tot_s[1], 1), yx_peers, 2)
-
-    transpose_product(1, at_start, at_sent)
-    step = next_step(step, collect("sum_yx", 8, tot_s[2], 15), 0)
+        spread("sum_row", 7, collect("sum_col", 0, value, 7), (row_peer, NR), 1)
+
+    transpose_product(1, at_start)
+    step = next_step(step, collect("sum_row", 7, tot_s[1], 31), 0)
     x_next = next_primal(x_now, step, pull(1))
     gather_x(2, x_next)
     x_link = next_links(x_link, step, link_pull(1))
     beside = from_links(x_link)
     x_next = patched(x_next, x_link)
-    x_out[...] = x_next
+    results[0] = x_next
+    out_x = pltpu.make_async_copy(results.at[0], x_out, small_sem.at[13])
+    out_x.start()
     forward_product(2, gathered_x(2), *beside)
     image_new = image(2)
     y_next = next_dual(y_now, step, image_old, image_new)
-    y_out[...] = y_next
+    results[1] = y_next
+    out_y = pltpu.make_async_copy(results.at[1], y_out, small_sem.at[14])
+    out_y.start()
     value = sums(x_next - x_now, y_next - y_now, image_new - image_old)
-    spread("last_z", 23, value, side_peers, 3)
-    value = collect("last_z", 23, value, 15)
-    spread("last_yx", 38, value, yx_peers, 4)
-    value = collect("last_yx", 38, value, 15)
+    spread("last_z", 38, value, side_peers, 2)
+    value = collect("last_z", 38, value, 15)
+    spread("last_yx", 53, value, yx_peers, 3)
+    value = collect("last_yx", 53, value, 15)
     s_out[...] = next_step(step, value, 1)
 
+    out_x.wait()
+    out_y.wait()
     for name, ref in pending:
         total(name, ref).wait_send()
 
@@ -556,12 +563,14 @@
             jax.ShapeDtypeStruct((1, 1), F32),
         ),
         in_specs=[hbm] * 15,
-        out_specs=(vmem, vmem, vmem),
+        out_specs=(hbm, hbm, vmem),
         scratch_shapes=[
             pltpu.VMEM((GROUPS * 8 * T, T), F32),
             [pltpu.VMEM((1, m), jnp.int32) for m in (SLOTS, SLOTS, 1, LS, LS, LS)]
             + [pltpu.VMEM((1, 1), F32)] * 2,
             pltpu.VMEM((3, OWN, 128), F32),
+            pltpu.VMEM((GROUPS * 8 * T, T), BF16),
+            pltpu.VMEM((GROUPS * 8 * T, T), BF16),
             pltpu.VMEM((GROUPS * 8 * T, T), BF16),
             pltpu.VMEM((GROUPS * 8 * T, T), BF16),
             pltpu.VMEM((NR, 2 * OWN, 128), F32),
@@ -575,8 +584,8 @@
             [pltpu.VMEM((NC, m * OWN, 128), F32) for m in (2, 1, 1)],
             pltpu.VMEM((2, OWN, 128), F32),
             pltpu.VMEM((2, XR, 128), F32),
-            pltpu.VMEM((5, 8, 128), F32),
-            pltpu.VMEM((53 * 8, 128), F32),
+            pltpu.VMEM((4, 8, 128), F32),
+            pltpu.VMEM((68 * 8, 128), F32),
             pltpu.VMEM((YR, 128), BF16),
             pltpu.VMEM((XR, 128), BF16),
             pltpu.VMEM((80, YR), BF16),
@@ -587,8 +596,9 @@
             pltpu.VMEM((16, 128), BF16),
             pltpu.VMEM((GROUPS - 1, 16, T), F32),
             pltpu.VMEM((GROUPS - 1, 8, T), F32),
+            pltpu.VMEM((2, OWN, 128), F32),
             pltpu.SemaphoreType.DMA((CHUNKS,)),
-            pltpu.SemaphoreType.DMA((13,)),
+            pltpu.SemaphoreType.DMA((15,)),
             pltpu.SemaphoreType.DMA((n,)),
             pltpu.SemaphoreType.DMA((n,)),
         ],

time: 94.8 us -> 92.1 us (0.972)
  Pallas kernels: 87.6 us -> 84.9 us
    pallas_call x1, Pallas kernels: 87.6 us -> 84.9 us  [on_device(): pl.pallas_call(kernel, out_shape=(jax.ShapeDtypeStruct((OWN, 128), F32),...]
where the time goes in v1:
time: 92.1 us; the launch traced here: 91.8 us
  Pallas kernels  84.9 us (92%)
  between operations  4.34 us (5%)
  local copies, waits for them, and re-layouts  2.59 us (3%)
    pallas_call x1, Pallas kernels, on_device(): pl.pallas_call(kernel, out_shape=(jax.ShapeDtypeStruct((OWN, 128), F32),...  84.9 us
    unnamed x2, local copies, waits for them, and re-layouts  2.59 us

profile of v1, /device:TPU:1, one launch (start us, length us, event | category | flops | bytes accessed | tf_op | source)
XLA Modules:
  0.0 91.8 jit_solution(7635710607245614225)
XLA Ops:
  2.6 84.9 %pdhg.1 = (f32[16,128]{1,0:T(8,128)}, f32[16,128]{1,0:T(8,128)}, f32[1,1]{1,0:T(1,128)}) custom-call(f32[8192,256]{1,0:T(8,128)} %bitcast.19, f32[2048,256]{1,0:T(8,128)} %bitcast.20, s32[1,32]{1,0:T(1,128)} %bitcast.28, s32[1,32]{1,0:T(1,128)} %bitcast.29, s32[1,1]{1,0:T(1,128)S(6)} %copy.21.cnt, s32[1,8]{1,0:T(1,128)} %bitcast.30, s32[1,8]{1,0:T(1,128)} %bitcast.31, ...), custom_call_target="tpu_custom_call" | custom-call | tf_op jit(solution)/shard_map/pdhg/pallas_call | solution.py:558
  87.4 1.3 %copy.24 = f32[2048]{0:T(1024)} copy(f32[2048]{0:T(1024)} %bitcast.22) | data formatting | bytes 16384
  88.7 1.3 %copy.25 = f32[2048]{0:T(1024)} copy(f32[2048]{0:T(1024)} %bitcast.21) | data formatting | bytes 16384
